TPU v7x, 256 devices: a whole 4x4x8 slice. The times are simulated.
256 devices in a mesh: dap: 64 (over x, z, y_hi), head: 4 (over y_lo, core).
Axes of the slice: x: 4, y: 4 (y_hi: 2, y_lo: 2; y = y_hi * 2 + y_lo), z: 8, core: 2. Of those that a mesh axis runs over, the one named last changes fastest.
Arguments:
- pair: bfloat16 [1024, 1024, 128], P('dap'), may hold values from -600 to 600
- residue_mask: int32 [1024], replicated, may hold values 0 or 1
- chain_breaks: int32 [1024], replicated, may hold values 0 or 1
- w_query: bfloat16 [128, 128], P(None, 'head'), may hold values from -0.5 to 0.5
- w_key: bfloat16 [128, 128], P(None, 'head'), may hold values from -0.5 to 0.5
- w_value: bfloat16 [128, 128], P(None, 'head'), may hold values from -0.5 to 0.5
- w_gate: bfloat16 [128, 128], P(None, 'head'), may hold values from -0.5 to 0.5
- w_bias: bfloat16 [128, 4], P(None, 'head'), may hold values from -29 to 29
- w_out: bfloat16 [128, 128], P('head'), may hold values from -0.5 to 0.5
Outputs:
- update: bfloat16 [1024, 1024, 128], P('dap', None, 'head')
All inputs are finite; a program needn't handle non-finite values.
Results may differ from a plain program's by a relative error of at most 0.019.
Values may be sent and summed in bfloat16 or wider, within the bound.
No kernel may reach another device: no remote copies, remote signals or barrier semaphores. Data moves between devices by JAX's collectives and lax.ppermute only.
A program may use at most 64 MiB of HBM per device.

v0:
```python
import jax
import jax.numpy as jnp
from jax import lax
from jax.sharding import PartitionSpec as P

chain_penalty = 2.0
masked_score = -1000000000.0


def normalize(pair):
    x = pair.astype(jnp.float32)
    mean = jnp.mean(x, -1, keepdims=True)
    centered = x - mean
    variance = jnp.mean(centered * centered, -1, keepdims=True)
    return (centered * lax.rsqrt(variance + 1e-05)).astype(jnp.bfloat16)


def body(pair, residue_mask, chain_breaks, w_query, w_key, w_value, w_gate, w_bias, w_out):
    total = pair.shape[1]
    local_width = w_query.shape[1]
    local_heads = w_bias.shape[1]
    head_width = local_width // local_heads
    normed = normalize(pair)
    query = (
        jnp.dot(normed, w_query, preferred_element_type=jnp.float32) * head_width ** (-0.5)
    ).astype(jnp.bfloat16)
    keys = jnp.dot(normed, w_key, preferred_element_type=jnp.float32).astype(jnp.bfloat16)
    values = jnp.dot(normed, w_value, preferred_element_type=jnp.float32).astype(jnp.bfloat16)
    gate = jax.nn.sigmoid(jnp.dot(normed, w_gate, preferred_element_type=jnp.float32)).astype(
        jnp.bfloat16
    )
    bias_rows = jnp.einsum(
        "rnc,ch->hrn", normed, w_bias, preferred_element_type=jnp.float32
    ).astype(jnp.bfloat16)
    packed = jnp.concatenate([query, keys, values], axis=2)
    columns = lax.all_to_all(packed, "dap", split_axis=1, concat_axis=0, tiled=True)
    bias_full = lax.all_gather(bias_rows, "dap", axis=1, tiled=True)
    chain = jnp.cumsum(chain_breaks)
    penalty = jnp.where(chain[:, None] == chain[None, :], 0.0, -chain_penalty).astype(jnp.float32)
    keep = residue_mask[:, None] > 0

    def attend(index):
        column = lax.dynamic_index_in_dim(columns, index, 1, keepdims=False)
        q = column[:, :local_width].reshape(total, local_heads, head_width)
        k = column[:, local_width : 2 * local_width].reshape(total, local_heads, head_width)
        v = column[:, 2 * local_width : 3 * local_width].reshape(total, local_heads, head_width)
        scores = (
            jnp.einsum("khc,ihc->hki", k, q, preferred_element_type=jnp.float32)
            + bias_full.astype(jnp.float32)
            + penalty
        )
        scores = jnp.where(keep, scores, masked_score)
        top = jnp.max(scores, axis=1, keepdims=True)
        expo = jnp.exp(scores - top)
        weights = (expo / jnp.sum(expo, axis=1, keepdims=True)).astype(jnp.bfloat16)
        result = jnp.einsum("hki,khc->ihc", weights, v, preferred_element_type=jnp.float32)
        result = result.astype(jnp.bfloat16).reshape(total, local_width)
        return result

    attended = lax.map(attend, jnp.arange(columns.shape[1], dtype=jnp.int32))
    returned = lax.all_to_all(attended, "dap", split_axis=1, concat_axis=0, tiled=True)
    returned = jnp.swapaxes(returned, 0, 1)
    gated = (gate.astype(jnp.float32) * returned.astype(jnp.float32)).astype(jnp.bfloat16)
    term = jnp.dot(gated, w_out, preferred_element_type=jnp.float32)
    update = lax.psum_scatter(term, "head", scatter_dimension=2, tiled=True)
    return update.astype(jnp.bfloat16)


def solution(mesh):
    placed = (
        P("dap", None, None),
        P(),
        P(),
        P(None, "head"),
        P(None, "head"),
        P(None, "head"),
        P(None, "head"),
        P(None, "head"),
        P("head", None),
    )
    return jax.shard_map(
        body, mesh=mesh, in_specs=placed, out_specs=P("dap", None, "head"), check_vma=False
    )
```

profile of v0, /device:TPU:1, one launch (start us, length us, event | category | flops | bytes accessed | tf_op | source)
XLA Modules:
  0.0 477.1 jit_solution(2367408037299537434)
XLA Ops:
  6.5 3.5 convert_reduce_fusion
  10.1 4.7 fusion.14
  14.9 6.0 %multiply_convert_fusion = bf16[16,1024,32]{1,2,0:T(8,128)(2,1)S(1)} fusion(bf16[128,32]{0,1:T(8,128)(2,1)S(1)} %copy-done.4, bf16[16,1024,128]{2,1,0:T(8,128)(2,1)S(1)} %copy-done.1, f32[16,1024]{1,0:T(8,128)S(1)} %add_rsqrt_fusion, f32[16,1024]{1,0:T(8,128)S(1)} %broadcast_multiply_fusion), kind=kOutput, calls=%fused_computation.24 | convolution fusion | flops 143654912 | bytes 5382144 | tf_op jit(solution)/shard_map/dot_general | solution.py:25
  20.9 6.0 %convolution_convert_fusion.1 = bf16[16,1024,32]{1,2,0:T(8,128)(2,1)S(1)} fusion(bf16[128,32]{0,1:T(8,128)(2,1)S(1)} %copy-done.5, bf16[16,1024,128]{2,1,0:T(8,128)(2,1)S(1)} %copy-done.1, f32[16,1024]{1,0:T(8,128)S(1)} %add_rsqrt_fusion, f32[16,1024]{1,0:T(8,128)S(1)} %broadcast_multiply_fusion), kind=kOutput, calls=%fused_computation.27 | convolution fusion | flops 143130624 | bytes 5382144 | tf_op jit(solution)/shard_map/dot_general | solution.py:27
  26.9 6.0 %convolution_convert_fusion = bf16[16,1024,32]{1,2,0:T(8,128)(2,1)S(1)} fusion(bf16[128,32]{0,1:T(8,128)(2,1)S(1)} %copy-done.6, bf16[16,1024,128]{2,1,0:T(8,128)(2,1)S(1)} %copy-done.1, f32[16,1024]{1,0:T(8,128)S(1)} %add_rsqrt_fusion, f32[16,1024]{1,0:T(8,128)S(1)} %broadcast_multiply_fusion), kind=kOutput, calls=%fused_computation.26 | convolution fusion | flops 143130624 | bytes 5382144 | tf_op jit(solution)/shard_map/dot_general | solution.py:28
  33.2 5.0 %copy.30 = bf16[16,1024,96]{2,0,1:T(8,128)(2,1)} copy(bf16[16,1024,96]{1,2,0:T(8,128)(2,1)S(1)} %pad_maximum_fusion) | data formatting | bytes 6291456 | tf_op jit(solution)/shard_map/concatenate | solution.py:35
  38.1 15.5 %all-to-all-start = ((bf16[16,1024,96]{2,0,1:T(8,128)(2,1)}), bf16[16,1024,96]{2,0,1:T(8,128)(2,1)}, u32[]{:S(2)}, u32[]{:S(2)}) async-start(bf16[16,1024,96]{2,0,1:T(8,128)(2,1)} %copy.30), calls=%async_computation | async-start | bytes 8388608 | tf_op jit(solution)/shard_map/all_to_all | solution.py:36
  53.7 6.3 %fusion.25 = bf16[1,16,1024]{2,0,1:T(2,128)(2,1)S(1)} fusion(bf16[128,1]{0,1:T(2,128)(2,1)S(1)} %copy-done.8, bf16[16,1024,128]{2,1,0:T(8,128)(2,1)} %param.11, f32[16,1024]{1,0:T(8,128)S(1)} %add_rsqrt_fusion, f32[16,1024]{1,0:T(8,128)S(1)} %broadcast_multiply_fusion), kind=kOutput, calls=%fused_computation.41 | convolution fusion | flops 12582912 | bytes 4358400 | tf_op jit(solution)/shard_map/rnc,ch->hrn/dot_general | solution.py:32
  61.6 89.4 %all-to-all-done = bf16[16,1024,96]{2,0,1:T(8,128)(2,1)} async-done(((bf16[16,1024,96]{2,0,1:T(8,128)(2,1)}), bf16[16,1024,96]{2,0,1:T(8,128)(2,1)}, u32[]{:S(2)}, u32[]{:S(2)}) %all-to-all-start) | async-done | bytes 3145760 | tf_op jit(solution)/shard_map/all_to_all | solution.py:36
  151.0 5.2 %copy.32 = bf16[64,16,16,96]{3,2,1,0:T(8,128)(2,1)} copy(bf16[64,16,16,96]{3,1,2,0:T(8,128)(2,1)} %bitcast.6) | data formatting | bytes 6291456 | tf_op jit(solution)/shard_map/all_to_all | solution.py:36
  156.2 5.5 %copy.33 = bf16[1024,16,96]{0,2,1:T(8,128)(2,1)S(1)} copy(bf16[1024,16,96]{2,1,0:T(8,128)(2,1)} %bitcast.68) | data formatting | bytes 6291456
  161.8 23.9 %all-gather.3.cloned.1.call-done = bf16[1024,1024]{1,0:T(8,128)(2,1)} async-done(((bf16[16,1024]{1,0:T(8,128)(2,1)}), bf16[1024,1024]{1,0:T(8,128)(2,1)}) %all-gather.3.cloned.1.call-update) | async-done | bytes 2097168 | tf_op jit(solution)/shard_map/all_gather | solution.py:37
  185.6 119.5 %while.11 = (s32[]{:T(128)}, bf16[16,1024,32]{1,2,0:T(8,128)(2,1)}, s32[16]{0:T(128)S(1)}, bf16[1024,16,96]{0,2,1:T(8,128)(2,1)S(1)}, pred[1024,1]{0,1:T(4,128)(...) while((s32[]{:T(128)}, bf16[16,1024,32]{1,2,0:T(8,128)(2,1)}, ...), condition=%wide.region_7.8_spmd.clone, body=%wide.region_4.7_spmd.clone.sunk | while | flops 146831360 | bytes 15367340 | solution.py:60
  203.3 2.7 fusion.40
  305.2 5.9 %copy.34 = bf16[16,1024,32]{2,0,1:T(8,128)(2,1)} copy(bf16[16,1024,32]{1,2,0:T(8,128)(2,1)} %get-tuple-element.42) | data formatting | bytes 2097152 | tf_op jit(solution)/shard_map/while | solution.py:60
  311.0 6.4 %reshape.116 = bf16[64,2,4096]{2,1,0:T(2,128)(2,1)S(1)} reshape(bf16[1024,16,32]{2,1,0:T(8,128)(2,1)} %bitcast.66) | data formatting | bytes 2097152
  317.4 32.9 %all_to_all.27 = bf16[64,2,4096]{2,1,0:T(2,128)(2,1)S(1)} all-to-all(bf16[64,2,4096]{2,1,0:T(2,128)(2,1)S(1)} %reshape.116), channel_id=1, replica_groups=mesh['dap'=64,'head'=4] {'dap'}, dimensions={0} | all-to-all | bytes 2097152 | tf_op jit(solution)/shard_map/all_to_all | solution.py:61
  350.3 3.5 reshape.117
  353.9 4.4 copy.35
  358.3 4.1 copy.36
  362.4 7.8 %copy.37 = f32[64,16,16,32]{3,2,1,0:T(8,128)} copy(f32[64,16,16,32]{3,2,0,1:T(8,128)} %bitcast.65) | data formatting | bytes 4194304 | tf_op jit(solution)/shard_map/convert_element_type | solution.py:63
  370.2 5.1 %copy.38 = f32[1024,16,32]{0,2,1:T(8,128)S(1)} copy(f32[1024,16,32]{2,1,0:T(8,128)} %bitcast.64) | data formatting | bytes 4194304 | tf_op jit(solution)/shard_map/convert_element_type | solution.py:63
  375.4 9.8 %fusion.17 = f32[16,1024,128]{1,2,0:T(8,128)} fusion(f32[1024,16,32]{0,2,1:T(8,128)S(1)} %copy.38, bf16[32,128]{1,0:T(8,128)(2,1)S(1)} %copy-done, bf16[128,32]{0,1:T(8,128)(2,1)S(1)} %copy-done.7, bf16[16,1024,128]{2,1,0:T(8,128)(2,1)} %param.11, f32[16,1024]{1,0:T(8,128)S(1)} %add_rsqrt_fusion, f32[16,1024]{1,0:T(8,128)S(1)} %broadcast_multiply_fusion), kind=kOutput, calls=%fused_computation.28 | convolution fusion | flops 280494080 | bytes 14827520 | tf_op jit(solution)/shard_map/dot_general | solution.py:64
  385.2 82.3 %reduce-scatter.2.cloned.1.call-done = f32[16,1024,32]{1,2,0:T(8,128)} async-done(((f32[16,1024,128]{1,2,0:T(8,128)}), f32[16,1024,32]{1,2,0:T(8,128)}) %reduce-scatter.2.cloned.1.call-update) | async-done | bytes 2097168 | tf_op jit(solution)/shard_map/reduce_scatter | solution.py:65
  (131 shorter events, 88.9 us)
Async XLA Ops:
  6.5 368.8 %copy-start = (bf16[32,128]{1,0:T(8,128)(2,1)S(1)}, bf16[32,128]{1,0:T(8,128)(2,1)}, u32[]{:S(2)}) copy-start(bf16[32,128]{1,0:T(8,128)(2,1)} %param.19) | copy-start | bytes 24580
  6.5 3.5 copy-start.1
  6.5 8.3 %copy-start.4 = (bf16[128,32]{0,1:T(8,128)(2,1)S(1)}, bf16[128,32]{0,1:T(8,128)(2,1)}, u32[]{:S(2)}) copy-start(bf16[128,32]{0,1:T(8,128)(2,1)} %param.14) | copy-start | bytes 24580
  14.8 6.0 %copy-start.5 = (bf16[128,32]{0,1:T(8,128)(2,1)S(1)}, bf16[128,32]{0,1:T(8,128)(2,1)}, u32[]{:S(2)}) copy-start(bf16[128,32]{0,1:T(8,128)(2,1)} %param.15) | copy-start | bytes 24580
  20.9 6.0 %copy-start.6 = (bf16[128,32]{0,1:T(8,128)(2,1)S(1)}, bf16[128,32]{0,1:T(8,128)(2,1)}, u32[]{:S(2)}) copy-start(bf16[128,32]{0,1:T(8,128)(2,1)} %param.16) | copy-start | bytes 24580
  38.1 15.6 %copy-start.8 = (bf16[128,1]{0,1:T(2,128)(2,1)S(1)}, bf16[128,1]{0,1:T(2,128)(2,1)}, u32[]{:S(2)}) copy-start(bf16[128,1]{0,1:T(2,128)(2,1)} %param.18) | copy-start | bytes 772
  38.1 112.8 %all-to-all-start = ((bf16[16,1024,96]{2,0,1:T(8,128)(2,1)}), bf16[16,1024,96]{2,0,1:T(8,128)(2,1)}, u32[]{:S(2)}, u32[]{:S(2)}) async-start(bf16[16,1024,96]{2,0,1:T(8,128)(2,1)} %copy.30), calls=%async_computation | async-start | bytes 8388608 | tf_op jit(solution)/shard_map/all_to_all | solution.py:36
  53.7 7.3 %copy-start.2 = (s32[1024]{0:T(1024)S(1)}, s32[1024]{0:T(1024)}, u32[]{:S(2)}) copy-start(s32[1024]{0:T(1024)} %param.12) | copy-start | bytes 12292
  53.7 7.3 %copy-start.3 = (s32[1024]{0:T(1024)S(1)}, s32[1024]{0:T(1024)}, u32[]{:S(2)}) copy-start(s32[1024]{0:T(1024)} %param.13) | copy-start | bytes 12292
  53.7 132.0 %all-gather.3.cloned.1.call-start = ((), (), s32[]{:S(2)}) async-start(), calls=%async_computation.4 | async-start | bytes 2129920 | tf_op jit(solution)/shard_map/all_gather | solution.py:37
  60.7 406.8 %reduce-scatter.2.cloned.1.call-start = ((), (), s32[]{:S(2)}) async-start(), calls=%async_computation.3 | async-start | bytes 10485760 | tf_op jit(solution)/shard_map/reduce_scatter | solution.py:65
  370.2 5.2 %copy-start.7 = (bf16[128,32]{0,1:T(8,128)(2,1)S(1)}, bf16[128,32]{0,1:T(8,128)(2,1)}, u32[]{:S(2)}) copy-start(bf16[128,32]{0,1:T(8,128)(2,1)} %param.17) | copy-start | bytes 24580
Sparse Core Ops, SparseCore 0:
  60.8 124.7 all-gather.2
  385.3 82.1 reduce-scatter.1
where the time goes:
time: 479 us; the launch traced here: 477 us
  waiting for transfers between devices  196 us (41%)
  matrix products  100 us (21%)
  local copies, waits for them, and re-layouts  64.5 us (13%)
  blocking collectives  32.9 us (7%)
  loops' own time  32.5 us (7%)
  other arithmetic  22 us (5%)
  starting transfers between devices  15.8 us (3%)
  between operations  13.6 us (3%)
    all_to_all x1, waiting for transfers between devices, body(): lax.all_to_all(packed, 'dap', split_axis=1, concat_axis=0, tiled=True)  89.4 us
    reduce_scatter x1, waiting for transfers between devices, body(): update = lax.psum_scatter(term, 'head', scatter_dimension=2, tiled=True)  82.3 us
    dot_general x16, matrix products, attend(): jnp.einsum('khc,ihc->hki', k, q, preferred_element_type=jnp.float32)  43.5 us
    all_to_all x1, blocking collectives, body(): lax.all_to_all(attended, 'dap', split_axis=1, concat_axis=0, tiled=True)  32.9 us
    another operation x1, loops' own time, body(): attended = lax.map(attend, jnp.arange(columns.shape[1], dtype=jnp.int32))  32.5 us
    all_gather x1, waiting for transfers between devices, body(): bias_full = lax.all_gather(bias_rows, 'dap', axis=1, tiled=True)  23.9 us
    dot_general x16, matrix products, attend(): jnp.einsum('hki,khc->ihc', weights, v, preferred_element_type=jnp.float32)  22.5 us
    convert_element_type x3, local copies, waits for them, and re-layouts, body(): returned.astype(jnp.float32)  17 us
  transfers between devices with their start and end apart: 3, of which 3 were waited for; matrix products, arithmetic and copies ran while one was open for 4% of the time, Pallas kernels for 0%

commit v1 on v0

v1 whole, which is shorter than its diff:
```python
import functools
import math

import jax
import jax.numpy as jnp
from jax import lax
from jax.experimental import pallas as pl
from jax.experimental.pallas import tpu as pltpu
from jax.sharding import PartitionSpec as P

bf16 = jnp.bfloat16
f32 = jnp.float32

N = 1024
C = 128
HEADS = 4
WIDTH = 32
NX, NZ, NY = 4, 8, 2
DAP = NX * NZ * NY
ROWS = N // DAP
COLS = N // (DAP * HEADS)
TILE = 256
LOG2E = math.log2(math.e)
PENALTY = -2.0 * LOG2E
MASKED = -1e9 * LOG2E
NT = (((1,), (1,)), ((), ()))
TN = (((0,), (0,)), ((), ()))


def dot(a, b, dims=(((1,), (0,)), ((), ()))):
    return lax.dot_general(a, b, dims, preferred_element_type=f32)


def norm_kernel(head_ref, pair_ref, normed_ref, send_ref):
    x = pair_ref[0].astype(f32)
    mean = jnp.mean(x, -1, keepdims=True)
    centered = x - mean
    variance = jnp.mean(centered * centered, -1, keepdims=True)
    normed_ref[0] = (centered * lax.rsqrt(variance + 1e-05)).astype(bf16)
    for c in range(COLS):
        start = pl.multiple_of(c * HEADS * DAP + head_ref[0] * DAP, DAP)
        send_ref[c, 0] = normed_ref[0, pl.ds(start, DAP), :]


def norm_call(pair, head):
    return pl.pallas_call(
        norm_kernel,
        grid_spec=pltpu.PrefetchScalarGridSpec(
            num_scalar_prefetch=1,
            grid=(ROWS,),
            in_specs=[pl.BlockSpec((1, N, C), lambda r, h: (r, 0, 0))],
            out_specs=[
                pl.BlockSpec((1, N, C), lambda r, h: (r, 0, 0)),
                pl.BlockSpec((COLS, 1, DAP, C), lambda r, h: (0, r, 0, 0)),
            ],
        ),
        out_shape=[
            jax.ShapeDtypeStruct((ROWS, N, C), bf16),
            jax.ShapeDtypeStruct((COLS, ROWS, DAP, C), bf16),
        ],
        name="norm",
    )(head, pair)


def bias_kernel(normed_ref, w_ref, out_ref):
    rows = normed_ref.shape[0]
    for r in range(rows):
        b = dot(w_ref[...], normed_ref[r], NT)
        out_ref[0, pl.ds(r, 1), :] = b[0:1].astype(bf16)
        out_ref[1, pl.ds(r, 1), :] = b[1:2].astype(bf16)


def bias_call(normed, w_two):
    return pl.pallas_call(
        bias_kernel,
        in_specs=[pl.BlockSpec(memory_space=pltpu.VMEM)] * 2,
        out_specs=pl.BlockSpec(memory_space=pltpu.VMEM),
        out_shape=jax.ShapeDtypeStruct((2, ROWS, N), bf16),
        compiler_params=pltpu.CompilerParams(vmem_limit_bytes=32 * 2**20),
        name="bias",
    )(normed, w_two)


def attend_kernel(
    x_ref, recv_ref, keep_ref, chain_col_ref, chain_row_ref, w_ref, wout_ref,
    b0, b1, b2, b3, b4, b5, b6, b7, out_ref, k_scr, q_scr, v_scr, g_scr, comb, s_scr, gated,
):
    pieces = ((b0, b1, b2, b3), (b4, b5, b6, b7))
    tile = pl.program_id(0)
    chunk_rows = N // NX
    per_chunk = DAP // NX

    @pl.when(tile == 0)
    def _():
        def project(c, carry):
            whole = recv_ref[:, c].reshape(N, C)
            q = (dot(w_ref[0].reshape(C, C), whole, NT) * WIDTH ** (-0.5)).astype(bf16)
            q = q.astype(f32) * LOG2E
            high = q.astype(bf16)
            low = (q - high.astype(f32)).astype(bf16)
            for h in range(HEADS):
                at = slice(h * WIDTH, (h + 1) * WIDTH)
                q_scr[c, h, 0:WIDTH] = high[at]
                q_scr[c, h, WIDTH : 2 * WIDTH] = low[at]
            gate = jax.nn.sigmoid(dot(w_ref[3].reshape(C, C), whole, NT))
            g_scr[c] = gate.astype(bf16)
            for s in range(NX):
                part = lax.rem(x_ref[0] + s, NX)
                rows = recv_ref[pl.ds(part * per_chunk, per_chunk), c].reshape(chunk_rows, C)
                here = pl.ds(s * chunk_rows, chunk_rows)
                for p in range(2):
                    wk = jnp.concatenate(
                        [w_ref[1, 2 * p], w_ref[1, 2 * p], w_ref[1, 2 * p + 1], w_ref[1, 2 * p + 1]], 0
                    )
                    k_scr[p, c, here] = (dot(rows, wk, NT) * keep_ref[part]).astype(bf16)
                v = dot(w_ref[2].reshape(C, C), rows, NT).astype(bf16)
                ones = jnp.where(
                    lax.broadcasted_iota(jnp.int32, (16, chunk_rows), 0) == 0, 1.0, 0.0
                ).astype(bf16)
                for h in range(HEADS):
                    v_scr[c, h, 0:WIDTH, here] = v[h * WIDTH : (h + 1) * WIDTH]
                    v_scr[c, h, WIDTH : WIDTH + 16, here] = ones
            return carry

        lax.fori_loop(0, COLS, project, 0)

    lanes = pl.ds(pl.multiple_of(tile * TILE, TILE), TILE)
    zeros = jnp.zeros((2 * WIDTH, TILE), bf16)
    for h in range(HEADS):
        for s in range(NX):
            part = lax.rem(x_ref[0] + s, NX)
            same = chain_col_ref[part] == chain_row_ref[0:1, :]
            term = pieces[h // 2][s][h % 2].astype(f32) * LOG2E + jnp.where(same, 0.0, PENALTY)
            comb[s] = jnp.where(keep_ref[part] > 0, term, MASKED)

        def column(c, carry, h=h):
            q = q_scr[c, h, :, lanes]
            q = jnp.concatenate([q, zeros] if h % 2 == 0 else [zeros, q], 0)
            top = None
            for s in range(NX):
                k = k_scr[h // 2, c, pl.ds(s * chunk_rows, chunk_rows)]
                scores = dot(k, q) + comb[s]
                s_scr[s] = scores
                high = jnp.max(scores.reshape(chunk_rows // 8, 8, TILE), 0)
                top = high if top is None else jnp.maximum(top, high)
            top = jnp.max(top, 0, keepdims=True)
            total = jnp.zeros((WIDTH + 16, TILE), f32)
            for s in range(NX):
                weights = jnp.exp2(s_scr[s] - top).astype(bf16)
                total = total + dot(v_scr[c, h, :, pl.ds(s * chunk_rows, chunk_rows)], weights)
            attended = (total[0:WIDTH] / total[WIDTH : WIDTH + 1]).astype(bf16).astype(f32)
            gate = g_scr[c, h * WIDTH : (h + 1) * WIDTH, lanes].astype(f32)
            gated[c, h * WIDTH : (h + 1) * WIDTH] = (gate * attended).astype(bf16)
            return carry

        lax.fori_loop(0, COLS, column, 0)
    joined = gated[...].reshape(COLS * C, TILE)
    for o in range(HEADS):
        out_ref[o] = dot(joined, wout_ref[o], TN).astype(bf16)


def attend_call(x, recv, keep, chain_col, chain_row, weights, w_out, pieces):
    whole = lambda shape: pl.BlockSpec(shape, lambda t, x: (0,) * len(shape))
    return pl.pallas_call(
        attend_kernel,
        grid_spec=pltpu.PrefetchScalarGridSpec(
            num_scalar_prefetch=1,
            grid=(N // TILE,),
            in_specs=[
                whole((DAP, COLS, ROWS, C)),
                whole((NX, N // NX, 1)),
                whole((NX, N // NX, 1)),
                pl.BlockSpec((8, TILE), lambda t, x: (0, t)),
                whole((4, HEADS, WIDTH, C)),
                whole((HEADS, COLS * C, C)),
            ]
            + [pl.BlockSpec((2, N // NX, TILE), lambda t, x: (0, 0, t))] * 8,
            out_specs=pl.BlockSpec((HEADS, TILE, C), lambda t, x: (0, t, 0)),
            scratch_shapes=[
                pltpu.VMEM((2, COLS, N, C), bf16),
                pltpu.VMEM((COLS, HEADS, 2 * WIDTH, N), bf16),
                pltpu.VMEM((COLS, HEADS, WIDTH + 16, N), bf16),
                pltpu.VMEM((COLS, C, N), bf16),
                pltpu.VMEM((NX, N // NX, TILE), f32),
                pltpu.VMEM((NX, N // NX, TILE), f32),
                pltpu.VMEM((COLS, C, TILE), bf16),
            ],
        ),
        out_shape=jax.ShapeDtypeStruct((HEADS, N, C), bf16),
        compiler_params=pltpu.CompilerParams(vmem_limit_bytes=48 * 2**20),
        name="attend",
    )(x, recv, keep, chain_col, chain_row, weights, w_out, *pieces)


def at(x, z, y):
    return (x % NX) * NZ * NY + (z % NZ) * NY + y % NY


def shift(dx, dz, dy):
    return [
        (at(x, z, y), at(x + dx, z + dz, y + dy))
        for x in range(NX) for z in range(NZ) for y in range(NY)
    ]


def send(value, dx, dz, dy):
    return lax.ppermute(value, "dap", shift(dx, dz, dy))


def gather_plane(rows, z, y):
    other = send(rows, 0, 0, 1)
    first = jnp.where(y == 0, rows, other)
    second = jnp.where(y == 0, other, rows)
    mine = jnp.concatenate([first, second], 1)
    up = down = mine
    got = {0: mine}
    for step in range(1, 4):
        up, down = send(up, 0, 1, 0), send(down, 0, -1, 0)
        got[NZ - step], got[step] = up, down
    got[4] = jnp.concatenate([send(up[:1], 0, 1, 0), send(down[1:], 0, -1, 0)], 0)
    ordered = jnp.concatenate([got[i] for i in range(NZ)] * 2, 1)
    start = (NZ - z) % NZ * (NY * ROWS)
    return lax.dynamic_slice_in_dim(ordered, start, NZ * NY * ROWS, 1)


def gather_bias(rows, z, y):
    plane = gather_plane(rows, z, y)
    left, right = send(plane, 1, 0, 0), send(plane, -1, 0, 0)
    far = jnp.concatenate([send(left[:1], 1, 0, 0), send(right[1:], -1, 0, 0)], 0)
    own = [plane, right, far, left]
    swap = [(h, h ^ 1) for h in range(HEADS)]
    return own + [lax.ppermute(piece, "head", swap) for piece in own]


def body(pair, residue_mask, chain_breaks, w_query, w_key, w_value, w_gate, w_bias, w_out):
    dap = lax.axis_index("dap").astype(jnp.int32)
    head = lax.axis_index("head").astype(jnp.int32)
    x, z, y = dap // (NZ * NY), dap // NY % NZ, dap % NY
    core = head % 2
    packed = jnp.concatenate(
        [w_query.T, w_key.T, w_value.T, w_gate.T, w_out, w_bias.T, jnp.zeros((15, C), bf16)], 0
    )
    packed = lax.all_gather(packed, "head", axis=0)
    packed = lax.dynamic_slice_in_dim(jnp.concatenate([packed, packed], 0), 2 * core, HEADS, 0)
    weights = jnp.swapaxes(packed[:, : 4 * WIDTH].reshape(HEADS, 4, WIDTH, C), 0, 1)
    full_out = packed[:, 4 * WIDTH : 5 * WIDTH].reshape(C, HEADS, WIDTH)
    eye = jnp.eye(COLS, dtype=bf16)
    spread = (
        jnp.transpose(full_out, (1, 0, 2))[:, None, :, None, :] * eye[None, :, None, :, None]
    ).reshape(HEADS, COLS * C, COLS * WIDTH)
    w_two = packed[:2, 5 * WIDTH]
    w_two = jnp.concatenate([w_two, jnp.zeros((14, C), bf16)], 0)

    normed, out = norm_call(pair, head[None])
    recv = lax.all_to_all(jnp.transpose(out, (2, 0, 1, 3)), "dap", 0, 0, tiled=True)
    pieces = gather_bias(bias_call(normed, w_two), z, y)

    chain = jnp.cumsum(chain_breaks).astype(jnp.int32)
    keep = (residue_mask > 0).astype(f32).reshape(NX, N // NX, 1)
    update = attend_call(
        x[None], recv, keep, chain.reshape(NX, N // NX, 1),
        jnp.broadcast_to(chain[None], (8, N)), weights, spread, pieces,
    )
    update = update.reshape(HEADS * DAP, ROWS, C)
    update = lax.all_to_all(update, ("head", "dap"), 0, 0, tiled=True)
    update = update.reshape(HEADS * DAP, ROWS, COLS, WIDTH)
    return jnp.transpose(update, (1, 2, 0, 3)).reshape(ROWS, N, WIDTH)


def solution(mesh):
    placed = (
        P("dap", None, None), P(), P(),
        P(None, "head"), P(None, "head"), P(None, "head"), P(None, "head"), P(None, "head"),
        P("head", None),
    )
    return jax.shard_map(
        body, mesh=mesh, in_specs=placed, out_specs=P("dap", None, "head"), check_vma=False
    )
```

time: 479 us -> 230 us (0.48)
  waiting for transfers between devices: 196 us -> 19.1 us
  matrix products: 100 us -> 0 us
  Pallas kernels: 0 us -> 66.1 us
  starting transfers between devices: 15.8 us -> 54.2 us
  loops' own time: 32.5 us -> 0 us
  local copies, waits for them, and re-layouts: 64.5 us -> 33.7 us
  blocking collectives: 32.9 us -> 51.5 us
  other arithmetic: 22 us -> 3.43 us
  between operations: 13.6 us -> 0.36 us
    dot_general x37 -> x0, matrix products: 100 us -> none  [the longest x16 43.5 us: attend(): jnp.einsum('khc,ihc->hki', k, q, preferred_element_type=jnp.float32)]
    all_to_all x1, waiting for transfers between devices: 89.4 us -> 0.01 us  [body(): lax.all_to_all(jnp.transpose(out, (2, 0, 1, 3)), 'dap', 0, 0, tiled=True)]
    reduce_scatter x1 -> x0, waiting for transfers between devices: 82.3 us -> none  [body(): update = lax.psum_scatter(term, 'head', scatter_dimension=2, tiled=True)]
    pallas_call x0 -> x3, Pallas kernels: none -> 66.1 us  [the longest x1 52.1 us: attend_call(): pl.pallas_call(attend_kernel, grid_spec=pltpu.PrefetchScalarGridSpec(num_...]
    ppermute x0 -> x17, starting transfers between devices: none -> 43.7 us  [the longest x4 25 us: gather_bias(): return own + [lax.ppermute(piece, 'head', swap) for piece in own]]
    another operation x1 -> x0, loops' own time: 32.5 us -> none  [body(): attended = lax.map(attend, jnp.arange(columns.shape[1], dtype=jnp.int32))]
    all_gather x1 -> x0, waiting for transfers between devices: 23.9 us -> none  [body(): bias_full = lax.all_gather(bias_rows, 'dap', axis=1, tiled=True)]
    ppermute x0 -> x17, waiting for transfers between devices: none -> 19.1 us  [the longest x13 19.1 us: send(): return lax.ppermute(value, 'dap', shift(dx, dz, dy))]
  transfers between devices with their start and end apart: 3 -> 18, of which waited for: 3 -> 6; matrix products, arithmetic and copies ran while one was open for 4% -> 11% of each run, Pallas kernels for 0% -> 0%
where the time goes in v1:
time: 230 us; the launch traced here: 228 us
  Pallas kernels  66.1 us (29%)
  starting transfers between devices  54.2 us (24%)
  blocking collectives  51.5 us (22%)
  local copies, waits for them, and re-layouts  33.7 us (15%)
  waiting for transfers between devices  19.1 us (8%)
  other arithmetic  3.43 us (1%)
    pallas_call x1, Pallas kernels, attend_call(): pl.pallas_call(attend_kernel, grid_spec=pltpu.PrefetchScalarGridSpec(num_...  52.1 us
    all_to_all x1, blocking collectives, body(): update = lax.all_to_all(update, ('head', 'dap'), 0, 0, tiled=True)  42.9 us
    ppermute x4, starting transfers between devices, gather_bias(): return own + [lax.ppermute(piece, 'head', swap) for piece in own]  25 us
    ppermute x13, waiting for transfers between devices, send(): return lax.ppermute(value, 'dap', shift(dx, dz, dy))  19.1 us
    ppermute x13, starting transfers between devices, send(): return lax.ppermute(value, 'dap', shift(dx, dz, dy))  18.8 us
    pallas_call x1, Pallas kernels, norm_call(): pl.pallas_call(norm_kernel, grid_spec=pltpu.PrefetchScalarGridSpec(num_sc...  12.8 us
    all_to_all x1, starting transfers between devices, body(): lax.all_to_all(jnp.transpose(out, (2, 0, 1, 3)), 'dap', 0, 0, tiled=True)  10.4 us
    all_gather x1, blocking collectives, body(): packed = lax.all_gather(packed, 'head', axis=0)  8.64 us
  transfers between devices with their start and end apart: 18, of which 6 were waited for; matrix products, arithmetic and copies ran while one was open for 11% of the time, Pallas kernels for 0%

profile of v1, /device:TPU:1, one launch (start us, length us, event | category | flops | bytes accessed | tf_op | source)
XLA Modules:
  0.0 228.4 jit_solution(17590709558227036268)
XLA Ops:
  0.0 4.3 %concatenate.22 = bf16[176,128]{1,0:T(8,128)(2,1)S(1)} concatenate(bf16[32,128]{1,0:T(8,128)(2,1)} %bitcast.47, bf16[32,128]{1,0:T(8,128)(2,1)} %bitcast.48, bf16[32,128]{1,0:T(8,128)(2,1)} %bitcast.49, bf16[32,128]{1,0:T(8,128)(2,1)} %bitcast.50, bf16[32,128]{1,0:T(8,128)(2,1)} %param.17, bf16[1,128]{1,0:T(2,128)(2,1)} %bitcast.52, bf16[15,128]{1,0:T(8,128)(2,1)S(1)} %broadcast_in_dim.21), dimensions={0} | concatenate | bytes 90112 | tf_op jit(solution)/shard_map/concatenate | solution.py:240
  4.3 8.6 %all-gather = bf16[704,128]{1,0:T(8,128)(2,1)S(1)} all-gather(bf16[176,128]{1,0:T(8,128)(2,1)S(1)} %concatenate.22), channel_id=2, replica_groups=mesh['dap'=64,'head'=4] {'head'}, dimensions={0}, use_global_device_ids=true | all-gather | bytes 225280 | tf_op jit(solution)/shard_map/all_gather | solution.py:243
  13.4 12.8 %norm.1 = (bf16[16,1024,128]{2,1,0:T(8,128)(2,1)}, bf16[4,16,64,128]{3,2,1,0:T(8,128)(2,1)}) custom-call(s32[1]{0:T(128)} %bitcast.1.head_ref, bf16[16,1024,128]{2,1,0:T(8,128)(2,1)} %pair_ref.1), custom_call_target="tpu_custom_call" | custom-call | tf_op jit(solution)/shard_map/norm/pallas_call | solution.py:46
  26.2 2.2 copy-done
  30.8 3.9 %collective-permute-done = bf16[2,16,1024]{2,1,0:T(8,128)(2,1)S(1)} collective-permute-done((bf16[2,16,1024]{2,1,0:T(8,128)(2,1)S(1)}, bf16[2,16,1024]{2,1,0:T(8,128)(2,1)S(1)}, u32[]{:S(2)}, u32[]{:S(2)}) %collective-permute-start) | collective-permute-done | bytes 65568 | tf_op jit(solution)/shard_map/ppermute | solution.py:207
  34.9 3.9 %collective-permute-start.1 = (bf16[2,32,1024]{2,1,0:T(8,128)(2,1)S(1)}, bf16[2,32,1024]{2,1,0:T(8,128)(2,1)S(1)}, u32[]{:S(2)}, u32[]{:S(2)}) collective-permute-start(bf16[2,32,1024]{2,1,0:T(8,128)(2,1)S(1)} %pad_maximum_fusion), channel_id=1, source_target_pairs={{0,56},{4,60},{8,0},{12,4},{16,8},{20,12},{24,16},{28,20},{32,24},... | collective-permute-start | bytes 393224 | tf_op jit(solution)/shard_map/ppermute | solution.py:207
  38.8 2.8 %collective-permute-done.4 = bf16[2,32,1024]{2,1,0:T(8,128)(2,1)S(1)} collective-permute-done((bf16[2,32,1024]{2,1,0:T(8,128)(2,1)S(1)}, bf16[2,32,1024]{2,1,0:T(8,128)(2,1)S(1)}, u32[]{:S(2)}, u32[]{:S(2)}) %collective-permute-start.4) | collective-permute-done | bytes 131104 | tf_op jit(solution)/shard_map/ppermute | solution.py:207
  41.6 2.7 %collective-permute-start.2 = (bf16[2,32,1024]{2,1,0:T(8,128)(2,1)S(1)}, bf16[2,32,1024]{2,1,0:T(8,128)(2,1)S(1)}, u32[]{:S(2)}, u32[]{:S(2)}) collective-permute-start(bf16[2,32,1024]{2,1,0:T(8,128)(2,1)S(1)} %collective-permute-done.1), channel_id=1, source_target_pairs={{0,56},{4,60},{8,0},{12,4},{16,8},{20,12},{24,16},{28,20},{32,24},... | collective-permute-start | bytes 393224 | tf_op jit(solution)/shard_map/ppermute | solution.py:207
  44.3 2.3 %collective-permute-done.5 = bf16[2,32,1024]{2,1,0:T(8,128)(2,1)S(1)} collective-permute-done((bf16[2,32,1024]{2,1,0:T(8,128)(2,1)S(1)}, bf16[2,32,1024]{2,1,0:T(8,128)(2,1)S(1)}, u32[]{:S(2)}, u32[]{:S(2)}) %collective-permute-start.5) | collective-permute-done | bytes 131104 | tf_op jit(solution)/shard_map/ppermute | solution.py:207
  46.6 2.7 %collective-permute-start.3 = (bf16[2,32,1024]{2,1,0:T(8,128)(2,1)S(1)}, bf16[2,32,1024]{2,1,0:T(8,128)(2,1)S(1)}, u32[]{:S(2)}, u32[]{:S(2)}) collective-permute-start(bf16[2,32,1024]{2,1,0:T(8,128)(2,1)S(1)} %collective-permute-done.2), channel_id=1, source_target_pairs={{0,56},{4,60},{8,0},{12,4},{16,8},{20,12},{24,16},{28,20},{32,24},... | collective-permute-start | bytes 393224 | tf_op jit(solution)/shard_map/ppermute | solution.py:207
  49.3 2.3 %collective-permute-done.6 = bf16[2,32,1024]{2,1,0:T(8,128)(2,1)S(1)} collective-permute-done((bf16[2,32,1024]{2,1,0:T(8,128)(2,1)S(1)}, bf16[2,32,1024]{2,1,0:T(8,128)(2,1)S(1)}, u32[]{:S(2)}, u32[]{:S(2)}) %collective-permute-start.6) | collective-permute-done | bytes 131104 | tf_op jit(solution)/shard_map/ppermute | solution.py:207
  51.7 2.7 %collective-permute-start.8 = (bf16[1,32,1024]{2,1,0:T(8,128)(2,1)S(1)}, bf16[1,32,1024]{2,1,0:T(8,128)(2,1)S(1)}, u32[]{:S(2)}, u32[]{:S(2)}) collective-permute-start(bf16[1,32,1024]{2,1,0:T(8,128)(2,1)S(1)} %slice.42), channel_id=1, source_target_pairs={{0,56},{4,60},{8,0},{12,4},{16,8},{20,12},{24,16},{28,20},{32,24},... | collective-permute-start | bytes 196616 | tf_op jit(solution)/shard_map/ppermute | solution.py:207
  60.7 10.4 %all-to-all-start = ((bf16[64,4,16,128]{3,2,1,0:T(8,128)(2,1)}), bf16[64,4,16,128]{3,2,1,0:T(8,128)(2,1)S(1)}, u32[]{:S(2)}, u32[]{:S(2)}) async-start(bf16[64,4,16,128]{3,2,1,0:T(8,128)(2,1)} %bitcast.40), calls=%async_computation | async-start | bytes 2097152 | tf_op jit(solution)/shard_map/all_to_all | solution.py:255
  71.1 6.2 %collective-permute-done.10.b3 = bf16[2,256,1024]{2,1,0:T(8,128)(2,1)} collective-permute-done((bf16[2,256,1024]{2,1,0:T(8,128)(2,1)S(1)}, bf16[2,256,1024]{2,1,0:T(8,128)(2,1)}, u32[]{:S(2)}, u32[]{:S(2)}) %collective-permute-start.10) | collective-permute-done | bytes 1048608 | tf_op jit(solution)/shard_map/ppermute | solution.py:207
  77.3 1.9 slice.43
  80.8 2.0 collective-permute-start.12
  83.1 18.8 %collective-permute-start.13 = (bf16[2,256,1024]{2,1,0:T(8,128)(2,1)S(1)}, bf16[2,256,1024]{2,1,0:T(8,128)(2,1)}, u32[]{:S(2)}, u32[]{:S(2)}) collective-permute-start(bf16[2,256,1024]{2,1,0:T(8,128)(2,1)S(1)} %constant_dynamic-slice_fusion.b0), channel_id=1, source_target_pairs={{0,1},{1,0},{2,3},{3,2},{4,5},{5,4},{6,7},{7,6},{8,9},{9,8},{10,11... | collective-permute-start | bytes 3145736 | tf_op jit(solution)/shard_map/ppermute | solution.py:232
  102.4 1.9 constant_dynamic-update-slice_fusion.17
  106.2 5.7 %collective-permute-start.15 = (bf16[2,256,1024]{2,1,0:T(8,128)(2,1)}, bf16[2,256,1024]{2,1,0:T(8,128)(2,1)}, u32[]{:S(2)}, u32[]{:S(2)}) collective-permute-start(bf16[2,256,1024]{2,1,0:T(8,128)(2,1)} %constant_dynamic-update-slice_fusion.16.b2), channel_id=1, source_target_pairs={{0,1},{1,0},{2,3},{3,2},{4,5},{5,4},{6,7},{7,6},{8,9},{9,8},{10,11... | collective-permute-start | bytes 3145736 | tf_op jit(solution)/shard_map/ppermute | solution.py:232
  119.4 2.0 mul.28
  121.4 2.0 copy.65
  126.5 1.9 broadcast_multiply_fusion.wout_ref
  131.5 52.1 %attend.1 = bf16[4,1024,128]{2,1,0:T(8,128)(2,1)S(1)} custom-call(s32[1]{0:T(128)} %bitcast.x_ref, bf16[64,4,16,128]{3,2,1,0:T(8,128)(2,1)S(1)} %all-to-all-done.recv_ref, f32[4,256,1]{2,1,0:T(8,128)S(1)} %copy-done.1, s32[4,256,1]{2,1,0:T(8,128)S(1)} %copy-done.2, s32[8,1024]{1,0:T(8,128)S(1)} %broadcast_in_dim.20.chain_row_ref, ...), custom_call_target="tpu_custom_call" | custom-call | tf_op jit(solution)/shard_map/attend/pallas_call | solution.py:164
  183.6 42.9 %all_to_all.10 = bf16[256,16,128]{2,1,0:T(8,128)(2,1)S(1)} all-to-all(bf16[256,16,128]{2,1,0:T(8,128)(2,1)S(1)} %bitcast.38), channel_id=1, replica_groups=mesh['dap'=64,'head'=4] {'head','dap'}, dimensions={0} | all-to-all | bytes 2097152 | tf_op jit(solution)/shard_map/all_to_all | solution.py:265
  (91 shorter events, 29.1 us)
Async XLA Ops:
  26.2 2.2 copy-start
  29.6 5.1 %collective-permute-start = (bf16[2,16,1024]{2,1,0:T(8,128)(2,1)S(1)}, bf16[2,16,1024]{2,1,0:T(8,128)(2,1)S(1)}, u32[]{:S(2)}, u32[]{:S(2)}) collective-permute-start(bf16[2,16,1024]{2,1,0:T(8,128)(2,1)S(1)} %bias.1), channel_id=1, source_target_pairs={{0,4},{4,0},{8,12},{12,8},{16,20},{20,16},{24,28},{28,24},{32,36},... | collective-permute-start | bytes 196616 | tf_op jit(solution)/shard_map/ppermute | solution.py:207
  34.8 6.8 %collective-permute-start.4 = (bf16[2,32,1024]{2,1,0:T(8,128)(2,1)S(1)}, bf16[2,32,1024]{2,1,0:T(8,128)(2,1)S(1)}, u32[]{:S(2)}, u32[]{:S(2)}) collective-permute-start(bf16[2,32,1024]{2,1,0:T(8,128)(2,1)S(1)} %pad_maximum_fusion), channel_id=1, source_target_pairs={{0,8},{4,12},{8,16},{12,20},{16,24},{20,28},{24,32},{28,36},{32,40... | collective-permute-start | bytes 393224 | tf_op jit(solution)/shard_map/ppermute | solution.py:207
  34.9 6.7 %collective-permute-start.1 = (bf16[2,32,1024]{2,1,0:T(8,128)(2,1)S(1)}, bf16[2,32,1024]{2,1,0:T(8,128)(2,1)S(1)}, u32[]{:S(2)}, u32[]{:S(2)}) collective-permute-start(bf16[2,32,1024]{2,1,0:T(8,128)(2,1)S(1)} %pad_maximum_fusion), channel_id=1, source_target_pairs={{0,56},{4,60},{8,0},{12,4},{16,8},{20,12},{24,16},{28,20},{32,24},... | collective-permute-start | bytes 393224 | tf_op jit(solution)/shard_map/ppermute | solution.py:207
  41.6 5.0 %collective-permute-start.5 = (bf16[2,32,1024]{2,1,0:T(8,128)(2,1)S(1)}, bf16[2,32,1024]{2,1,0:T(8,128)(2,1)S(1)}, u32[]{:S(2)}, u32[]{:S(2)}) collective-permute-start(bf16[2,32,1024]{2,1,0:T(8,128)(2,1)S(1)} %collective-permute-done.4), channel_id=1, source_target_pairs={{0,8},{4,12},{8,16},{12,20},{16,24},{20,28},{24,32},{28,36},{32,40... | collective-permute-start | bytes 393224 | tf_op jit(solution)/shard_map/ppermute | solution.py:207
  41.6 5.0 %collective-permute-start.2 = (bf16[2,32,1024]{2,1,0:T(8,128)(2,1)S(1)}, bf16[2,32,1024]{2,1,0:T(8,128)(2,1)S(1)}, u32[]{:S(2)}, u32[]{:S(2)}) collective-permute-start(bf16[2,32,1024]{2,1,0:T(8,128)(2,1)S(1)} %collective-permute-done.1), channel_id=1, source_target_pairs={{0,56},{4,60},{8,0},{12,4},{16,8},{20,12},{24,16},{28,20},{32,24},... | collective-permute-start | bytes 393224 | tf_op jit(solution)/shard_map/ppermute | solution.py:207
  46.6 5.0 %collective-permute-start.6 = (bf16[2,32,1024]{2,1,0:T(8,128)(2,1)S(1)}, bf16[2,32,1024]{2,1,0:T(8,128)(2,1)S(1)}, u32[]{:S(2)}, u32[]{:S(2)}) collective-permute-start(bf16[2,32,1024]{2,1,0:T(8,128)(2,1)S(1)} %collective-permute-done.5), channel_id=1, source_target_pairs={{0,8},{4,12},{8,16},{12,20},{16,24},{20,28},{24,32},{28,36},{32,40... | collective-permute-start | bytes 393224 | tf_op jit(solution)/shard_map/ppermute | solution.py:207
  46.6 5.0 %collective-permute-start.3 = (bf16[2,32,1024]{2,1,0:T(8,128)(2,1)S(1)}, bf16[2,32,1024]{2,1,0:T(8,128)(2,1)S(1)}, u32[]{:S(2)}, u32[]{:S(2)}) collective-permute-start(bf16[2,32,1024]{2,1,0:T(8,128)(2,1)S(1)} %collective-permute-done.2), channel_id=1, source_target_pairs={{0,56},{4,60},{8,0},{12,4},{16,8},{20,12},{24,16},{28,20},{32,24},... | collective-permute-start | bytes 393224 | tf_op jit(solution)/shard_map/ppermute | solution.py:207
  51.6 4.3 %collective-permute-start.7 = (bf16[1,32,1024]{2,1,0:T(8,128)(2,1)S(1)}, bf16[1,32,1024]{2,1,0:T(8,128)(2,1)S(1)}, u32[]{:S(2)}, u32[]{:S(2)}) collective-permute-start(bf16[1,32,1024]{2,1,0:T(8,128)(2,1)S(1)} %slice.41), channel_id=1, source_target_pairs={{0,8},{4,12},{8,16},{12,20},{16,24},{20,28},{24,32},{28,36},{32,40... | collective-permute-start | bytes 196616 | tf_op jit(solution)/shard_map/ppermute | solution.py:207
  51.7 4.3 %collective-permute-start.8 = (bf16[1,32,1024]{2,1,0:T(8,128)(2,1)S(1)}, bf16[1,32,1024]{2,1,0:T(8,128)(2,1)S(1)}, u32[]{:S(2)}, u32[]{:S(2)}) collective-permute-start(bf16[1,32,1024]{2,1,0:T(8,128)(2,1)S(1)} %slice.42), channel_id=1, source_target_pairs={{0,56},{4,60},{8,0},{12,4},{16,8},{20,12},{24,16},{28,20},{32,24},... | collective-permute-start | bytes 196616 | tf_op jit(solution)/shard_map/ppermute | solution.py:207
  56.0 3.0 %copy-start.4 = (bf16[4,16,64,128]{3,2,1,0:T(8,128)(2,1)S(1)}, bf16[4,16,64,128]{3,2,1,0:T(8,128)(2,1)}, u32[]{:S(2)}) copy-start(bf16[4,16,64,128]{3,2,1,0:T(8,128)(2,1)} %get-tuple-element.7) | copy-start | bytes 3145732
  56.3 21.0 %collective-permute-start.10 = (bf16[2,256,1024]{2,1,0:T(8,128)(2,1)S(1)}, bf16[2,256,1024]{2,1,0:T(8,128)(2,1)}, u32[]{:S(2)}, u32[]{:S(2)}) collective-permute-start(bf16[2,256,1024]{2,1,0:T(8,128)(2,1)S(1)} %constant_dynamic-slice_fusion.b0), channel_id=1, source_target_pairs={{0,64},{4,68},{8,72},{12,76},{16,80},{20,84},{24,88},{28,92},{32,9... | collective-permute-start | bytes 3145736 | tf_op jit(solution)/shard_map/ppermute | solution.py:207
  57.6 22.4 %collective-permute-start.9 = (bf16[2,256,1024]{2,1,0:T(8,128)(2,1)S(1)}, bf16[2,256,1024]{2,1,0:T(8,128)(2,1)S(1)}, u32[]{:S(2)}, u32[]{:S(2)}) collective-permute-start(bf16[2,256,1024]{2,1,0:T(8,128)(2,1)S(1)} %constant_dynamic-slice_fusion.b0), channel_id=1, source_target_pairs={{0,192},{4,196},{8,200},{12,204},{16,208},{20,212},{24,216},{28,22... | collective-permute-start | bytes 3145736 | tf_op jit(solution)/shard_map/ppermute | solution.py:207
  60.7 22.1 %copy-start.5 = (s32[1024]{0:T(1024)S(1)}, s32[1024]{0:T(1024)}, u32[]{:S(2)}) copy-start(s32[1024]{0:T(1024)} %param.11) | copy-start | bytes 12292
  60.7 67.7 %all-to-all-start = ((bf16[64,4,16,128]{3,2,1,0:T(8,128)(2,1)}), bf16[64,4,16,128]{3,2,1,0:T(8,128)(2,1)S(1)}, u32[]{:S(2)}, u32[]{:S(2)}) async-start(bf16[64,4,16,128]{3,2,1,0:T(8,128)(2,1)} %bitcast.40), calls=%async_computation | async-start | bytes 2097152 | tf_op jit(solution)/shard_map/all_to_all | solution.py:255
  79.2 23.2 %collective-permute-start.11 = (bf16[1,256,1024]{2,1,0:T(8,128)(2,1)}, bf16[1,256,1024]{2,1,0:T(8,128)(2,1)}, u32[]{:S(2)}, u32[]{:S(2)}) collective-permute-start(bf16[1,256,1024]{2,1,0:T(8,128)(2,1)} %slice.43), channel_id=1, source_target_pairs={{0,64},{4,68},{8,72},{12,76},{16,80},{20,84},{24,88},{28,92},{32,9... | collective-permute-start | bytes 1572872 | tf_op jit(solution)/shard_map/ppermute | solution.py:207
  80.8 23.6 %collective-permute-start.12 = (bf16[1,256,1024]{2,1,0:T(8,128)(2,1)}, bf16[1,256,1024]{2,1,0:T(8,128)(2,1)}, u32[]{:S(2)}, u32[]{:S(2)}) collective-permute-start(bf16[1,256,1024]{2,1,0:T(8,128)(2,1)} %slice.44), channel_id=1, source_target_pairs={{0,192},{4,196},{8,200},{12,204},{16,208},{20,212},{24,216},{28,22... | collective-permute-start | bytes 1572872 | tf_op jit(solution)/shard_map/ppermute | solution.py:207
  83.1 45.2 %collective-permute-start.13 = (bf16[2,256,1024]{2,1,0:T(8,128)(2,1)S(1)}, bf16[2,256,1024]{2,1,0:T(8,128)(2,1)}, u32[]{:S(2)}, u32[]{:S(2)}) collective-permute-start(bf16[2,256,1024]{2,1,0:T(8,128)(2,1)S(1)} %constant_dynamic-slice_fusion.b0), channel_id=1, source_target_pairs={{0,1},{1,0},{2,3},{3,2},{4,5},{5,4},{6,7},{7,6},{8,9},{9,8},{10,11... | collective-permute-start | bytes 3145736 | tf_op jit(solution)/shard_map/ppermute | solution.py:232
  101.9 26.5 %collective-permute-start.16 = (bf16[2,256,1024]{2,1,0:T(8,128)(2,1)}, bf16[2,256,1024]{2,1,0:T(8,128)(2,1)}, u32[]{:S(2)}, u32[]{:S(2)}) collective-permute-start(bf16[2,256,1024]{2,1,0:T(8,128)(2,1)} %collective-permute-done.10.b3), channel_id=1, source_target_pairs={{0,1},{1,0},{2,3},{3,2},{4,5},{5,4},{6,7},{7,6},{8,9},{9,8},{10,11... | collective-permute-start | bytes 3145736 | tf_op jit(solution)/shard_map/ppermute | solution.py:232
  102.0 26.4 %collective-permute-start.14 = (bf16[2,256,1024]{2,1,0:T(8,128)(2,1)S(1)}, bf16[2,256,1024]{2,1,0:T(8,128)(2,1)}, u32[]{:S(2)}, u32[]{:S(2)}) collective-permute-start(bf16[2,256,1024]{2,1,0:T(8,128)(2,1)S(1)} %collective-permute-done.9.b1), channel_id=1, source_target_pairs={{0,1},{1,0},{2,3},{3,2},{4,5},{5,4},{6,7},{7,6},{8,9},{9,8},{10,11... | collective-permute-start | bytes 3145736 | tf_op jit(solution)/shard_map/ppermute | solution.py:232
  106.2 22.2 %collective-permute-start.15 = (bf16[2,256,1024]{2,1,0:T(8,128)(2,1)}, bf16[2,256,1024]{2,1,0:T(8,128)(2,1)}, u32[]{:S(2)}, u32[]{:S(2)}) collective-permute-start(bf16[2,256,1024]{2,1,0:T(8,128)(2,1)} %constant_dynamic-update-slice_fusion.16.b2), channel_id=1, source_target_pairs={{0,1},{1,0},{2,3},{3,2},{4,5},{5,4},{6,7},{7,6},{8,9},{9,8},{10,11... | collective-permute-start | bytes 3145736 | tf_op jit(solution)/shard_map/ppermute | solution.py:232
  128.4 1.0 copy-start.1
  129.5 1.0 copy-start.2
  130.5 1.0 copy-start.3
